TPU v7x, 32 devices: a whole 2x2x4 slice. The times are simulated.
32 devices in a mesh: batch: 16 (over z, y, x), tp: 2 (over core).
Axes of the slice: x: 2, y: 2, z: 4, core: 2. Of those that a mesh axis runs over, the one named last changes fastest.
Arguments:
- tokens: bfloat16 [19456, 768], P('batch'), may hold values from -6 to 6
- seq_ids: int32 [19456], P('batch'), may hold values from 0 to 5, as said below
- cotangent: bfloat16 [19456, 768], P('batch'), may hold values from -6 to 6
- norm1_gain: float32 [768], replicated, may hold values from 0.1 to 1.9
- norm1_shift: float32 [768], replicated, may hold values from -3 to 3
- w_qkv: bfloat16 [768, 3, 768], P(None, None, 'tp'), may hold values from -0.21875 to 0.21875
- qv_bias: float32 [2, 768], P(None, 'tp'), may hold values from -3 to 3
- w_out: bfloat16 [768, 768], P('tp'), may hold values from -1.75 to 1.75
- out_bias: float32 [768], replicated, may hold values from -3 to 3
- norm2_gain: float32 [768], replicated, may hold values from 0.1 to 1.9
- norm2_shift: float32 [768], replicated, may hold values from -3 to 3
- w_in: bfloat16 [768, 3072], P(None, 'tp'), may hold values from -0.21875 to 0.21875
- in_bias: float32 [3072], P('tp'), may hold values from -3 to 3
- w_back: bfloat16 [3072, 768], P('tp'), may hold values from -0.109375 to 0.109375
- back_bias: float32 [768], replicated, may hold values from -3 to 3
Outputs:
- layer_out: bfloat16 [19456, 768], P('batch')
- tokens_grad: bfloat16 [19456, 768], P('batch')
- norm1_gain_grad: float32 [768], P('batch')
- norm1_shift_grad: float32 [768], P('batch')
- w_qkv_grad: float32 [768, 3, 768], P('batch', None, 'tp')
- qv_bias_grad: float32 [2, 768], P(None, ('tp', 'batch'))
- w_out_grad: float32 [768, 768], P('tp', 'batch')
- out_bias_grad: float32 [768], P('batch')
- norm2_gain_grad: float32 [768], P('batch')
- norm2_shift_grad: float32 [768], P('batch')
- w_in_grad: float32 [768, 3072], P('batch', 'tp')
- in_bias_grad: float32 [3072], P(('tp', 'batch'))
- w_back_grad: float32 [3072, 768], P('tp', 'batch')
- back_bias_grad: float32 [768], P('batch')
Inputs may be any that keep to these rules, and one draw needn't show every extreme that they name: `seq_ids`: in each aligned block of 1216 tokens, ids start at 0 and never fall; sequences of 608 tokens come first, then sequences of 228; the last may be cut by the block's end; some block holds only sequences of 228.
All inputs are finite; a program needn't handle non-finite values.
Results may differ from a plain program's by a relative error of at most 0.012.
Values sent between devices are 32-bit elements; how exact they have to be, the bound alone decides.
A program may use at most 192 MiB of HBM per device.

v0:
```python
import functools

import jax
import jax.numpy as jnp
from jax import lax
from jax.experimental import pallas as pl
from jax.experimental.pallas import tpu as pltpu
from jax.sharding import PartitionSpec as P

HEAD_DIM = 64
PAIR = 2 * HEAD_DIM
HALF = 608
TILE = 304
LANES = 384
VMEM_LIMIT = 63 << 20
WINDOW = 768
LOW = 448
ROWS = ((0, 128), (128, 128), (256, 128), (384, 128), (512, 96))
TILES = ((0, 256, 0, 608), (256, 352, 0, 688), (608, 256, 448, 1216), (864, 352, 608, 1216))
f32 = jnp.float32
bf16 = jnp.bfloat16


def params(mib):
    return pltpu.CompilerParams(vmem_limit_bytes=mib << 20)


def cost(flops, nbytes, trans=0):
    return pl.CostEstimate(flops=int(flops), bytes_accessed=int(nbytes), transcendentals=int(trans))


def nn(a, b):
    return jnp.dot(a, b, preferred_element_type=f32)


def nt(a, b):
    return lax.dot_general(a, b, (((1,), (1,)), ((), ())), preferred_element_type=f32)


def tn(a, b):
    return lax.dot_general(a, b, (((0,), (0,)), ((), ())), preferred_element_type=f32)


def standardize(values):
    center = values - jnp.mean(values, -1, keepdims=True)
    spread = jnp.mean(center * center, -1, keepdims=True)
    inv = lax.rsqrt(spread + 1e-06)
    return center * inv, inv


def norm_back(unit, inv, gain, grad):
    scaled = grad * gain
    return inv * (
        scaled
        - jnp.mean(scaled, -1, keepdims=True)
        - unit * jnp.mean(scaled * unit, -1, keepdims=True)
    )


def whole(shape):
    return pl.BlockSpec(shape, lambda *_: (0,) * len(shape))


def project_kernel(x_ref, gain_ref, shift_ref, w_ref, bias_ref, n_ref, q_ref, k_ref, v_ref):
    unit, _ = standardize(x_ref[...].astype(f32))
    normed = (unit * gain_ref[...] + shift_ref[...]).astype(bf16)
    n_ref[...] = normed
    scale = HEAD_DIM ** (-0.5)
    q_ref[...] = ((nn(normed, w_ref[0]) + bias_ref[0:1]).astype(bf16).astype(f32) * scale).astype(bf16)
    k_ref[...] = nn(normed, w_ref[1]).astype(bf16)
    v_ref[...] = (nn(normed, w_ref[2]) + bias_ref[1:2]).astype(bf16)


def project(tokens, gain, shift, w3, qv_bias):
    tok, dim = tokens.shape
    width = w3.shape[2]
    rows = lambda n: pl.BlockSpec((TILE, n), lambda i: (i, 0))
    out = jax.ShapeDtypeStruct((tok, width), bf16)
    return pl.pallas_call(
        project_kernel,
        grid=(tok // TILE,),
        in_specs=[rows(dim), whole((1, dim)), whole((1, dim)), whole(w3.shape), whole((2, width))],
        out_specs=[rows(dim), rows(width), rows(width), rows(width)],
        out_shape=[jax.ShapeDtypeStruct((tok, dim), bf16), out, out, out],
        compiler_params=params(60),
        cost_estimate=cost(2 * tok * dim * 3 * width, tok * (2 * dim + 3 * width) * 2 + w3.size * 2),
        name="project",
    )(tokens, gain, shift, w3, qv_bias)


def attend_kernel(half, q_ref, k_ref, v_ref, col_ref, row_ref, w_ref, *refs):
    o_ref, lse_ref, part_ref, *mask_refs = refs[-5:]
    step = pl.program_id(0)
    tiles = TILES[2 * half : 2 * half + 2]

    @pl.when(step == 0)
    def _():
        for (start, count, low, high), mask_ref in zip(tiles, mask_refs):
            at = start - half * HALF
            same = col_ref[at : at + count, :] == row_ref[:, low:high]
            mask_ref[...] = jnp.where(same, 0.0, -1000000000.0)

    first = lax.broadcasted_iota(jnp.int32, (1, PAIR), 1) < HEAD_DIM
    zero = jnp.zeros((), bf16)
    one = jnp.ones((), bf16)
    for tile, ((start, count, low, high), mask_ref) in enumerate(zip(tiles, mask_refs)):
        at = start - half * HALF
        rows = q_ref[at : at + count, :]
        keys = k_ref[low:high, :]
        values = v_ref[low:high, :]
        with_ones = (jnp.where(first, values, one), jnp.where(first, one, values))
        mask = mask_ref[...]
        outs, logs = [], []
        for head in range(2):
            own = jnp.where(first, rows, zero) if head == 0 else jnp.where(first, zero, rows)
            scores = nt(own, keys) + mask
            top = jnp.max(scores, -1, keepdims=True)
            expo = jnp.exp(scores - top).astype(bf16)
            mixed = nn(expo, with_ones[head])
            total = pltpu.roll(mixed, HEAD_DIM, 1)
            outs.append(mixed / total)
            logs.append(top + jnp.log(total))
        mixed = jnp.where(first, outs[0], outs[1]).astype(bf16)
        o_ref[at : at + count, :] = mixed
        turned = jnp.transpose(jnp.where(first, logs[0], logs[1]))
        lse_ref[tile, pl.ds(2 * step, 1), 0:count] = turned[0:1, :]
        lse_ref[tile, pl.ds(2 * step + 1, 1), 0:count] = turned[HEAD_DIM : HEAD_DIM + 1, :]
        part = nn(mixed, w_ref[...])

        @pl.when(step == 0)
        def _():
            part_ref[at : at + count, :] = part

        @pl.when(step > 0)
        def _():
            part_ref[at : at + count, :] += part


def attend(half, q, k, v, ids_col, ids_row, w_out, before=()):
    tok, width = q.shape
    dim = w_out.shape[1]
    pair_rows = pl.BlockSpec((HALF, PAIR), lambda p: (half, p))
    pair_all = pl.BlockSpec((tok, PAIR), lambda p: (0, p))
    tiles = TILES[2 * half : 2 * half + 2]
    return pl.pallas_call(
        functools.partial(attend_kernel, half),
        grid=(width // PAIR,),
        in_specs=[
            pair_rows,
            pair_all,
            pair_all,
            pl.BlockSpec((HALF, 1), lambda p: (half, 0)),
            whole((1, tok)),
            pl.BlockSpec((PAIR, dim), lambda p: (p, 0)),
        ]
        + [pl.BlockSpec(memory_space=pl.ANY)] * len(before),
        out_specs=[pair_rows, whole((2, 8, LANES)), whole((HALF, dim))],
        out_shape=[
            jax.ShapeDtypeStruct((tok, width), bf16),
            jax.ShapeDtypeStruct((2, 8, LANES), f32),
            jax.ShapeDtypeStruct((HALF, dim), f32),
        ],
        scratch_shapes=[pltpu.VMEM((count, high - low), f32) for _, count, low, high in tiles],
        input_output_aliases={6 + i: i for i in range(len(before))},
        compiler_params=params(60),
        cost_estimate=cost(16 * HALF * 650 * width, tok * width * 6 + HALF * dim * 4),
        name="attend",
    )(q, k, v, ids_col, ids_row, w_out, *before)


def hidden_kernel(x_ref, own_ref, peer_ref, ob_ref, gain_ref, shift_ref, w_ref, ib_ref, *refs):
    mid_ref, n_ref, hid_ref, slope_ref = refs[-4:]
    middle = x_ref[...].astype(f32) + (own_ref[...] + peer_ref[...]) + ob_ref[...]
    mid_ref[...] = middle
    unit, _ = standardize(middle)
    normed = (unit * gain_ref[...] + shift_ref[...]).astype(bf16)
    n_ref[...] = normed
    width = w_ref.shape[1]
    piece = 512
    c0 = 0.7978845608028654
    for at in range(0, width, piece):
        u = nn(normed, w_ref[:, at : at + piece]) + ib_ref[:, at : at + piece]
        sq = u * u
        t = jnp.tanh(u * (c0 + (c0 * 0.044715) * sq))
        cdf = 0.5 + 0.5 * t
        hid_ref[:, at : at + piece] = (u * cdf).astype(bf16)
        slope = cdf + (0.5 * u) * (1.0 - t * t) * (c0 + (3.0 * 0.044715 * c0) * sq)
        slope_ref[:, at : at + piece] = slope.astype(bf16)


def hidden_layer(half, tokens, own, peer, out_bias, gain, shift, w_in, in_bias, before=()):
    tok, dim = tokens.shape
    width = w_in.shape[1]
    per = HALF // TILE
    glob = lambda n: pl.BlockSpec((TILE, n), lambda i: (i + per * half, 0))
    loc = lambda n: pl.BlockSpec((TILE, n), lambda i: (i, 0))
    return pl.pallas_call(
        hidden_kernel,
        grid=(per,),
        in_specs=[
            glob(dim),
            loc(dim),
            loc(dim),
            whole((1, dim)),
            whole((1, dim)),
            whole((1, dim)),
            whole(w_in.shape),
            whole((1, width)),
        ]
        + [pl.BlockSpec(memory_space=pl.ANY)] * len(before),
        out_specs=[glob(dim), glob(dim), glob(width), glob(width)],
        out_shape=[
            jax.ShapeDtypeStruct((tok, dim), f32),
            jax.ShapeDtypeStruct((tok, dim), bf16),
            jax.ShapeDtypeStruct((tok, width), bf16),
            jax.ShapeDtypeStruct((tok, width), bf16),
        ],
        input_output_aliases={8 + i: i for i in range(len(before))},
        compiler_params=params(60),
        cost_estimate=cost(2 * HALF * dim * width, HALF * (dim * 16 + width * 4) + w_in.size * 2, HALF * width),
        name="hidden_layer",
    )(tokens, own, peer, out_bias, gain, shift, w_in, in_bias, *before)


def matmul_kernel(a_ref, b_ref, o_ref):
    o_ref[...] = nn(a_ref[...], b_ref[...])


def rows_matmul(a, b):
    tok, depth = a.shape
    width = b.shape[1]
    return pl.pallas_call(
        matmul_kernel,
        grid=(tok // TILE,),
        in_specs=[pl.BlockSpec((TILE, depth), lambda i: (i, 0)), whole(b.shape)],
        out_specs=pl.BlockSpec((TILE, width), lambda i: (i, 0)),
        out_shape=jax.ShapeDtypeStruct((tok, width), f32),
        compiler_params=params(60),
        cost_estimate=cost(2 * tok * depth * width, tok * (depth * 2 + width * 4) + b.size * 2),
        name="mlp_out",
    )(a, b)


def hidden_back_kernel(g_ref, slope_ref, wb_ref, wi_ref, du_ref, dn_ref, db_ref, gb_ref):
    step = pl.program_id(0)
    grad = g_ref[...]
    width = slope_ref.shape[1]
    piece = 512
    total = None
    sums = []
    for at in range(0, width, piece):
        back = nt(grad, wb_ref[at : at + piece, :])
        du = (back * slope_ref[:, at : at + piece].astype(f32)).astype(bf16)
        du_ref[:, at : at + piece] = du
        sums.append(jnp.sum(du.astype(f32), 0, keepdims=True))
    dn_ref[...] = nt(du_ref[...], wi_ref[...])

    @pl.when(step == 0)
    def _():
        db_ref[...] = jnp.zeros_like(db_ref)
        gb_ref[...] = jnp.zeros_like(gb_ref)

    for i, at in enumerate(range(0, width, piece)):
        db_ref[:, at : at + piece] += sums[i]
    gb_ref[...] += jnp.sum(grad.astype(f32), 0, keepdims=True)


def hidden_back(cotangent, slope, w_back, w_in):
    tok, dim = cotangent.shape
    width = slope.shape[1]
    rows = lambda n: pl.BlockSpec((TILE, n), lambda i: (i, 0))
    return pl.pallas_call(
        hidden_back_kernel,
        grid=(tok // TILE,),
        in_specs=[rows(dim), rows(width), whole(w_back.shape), whole(w_in.shape)],
        out_specs=[rows(width), rows(dim), whole((1, width)), whole((1, dim))],
        out_shape=[
            jax.ShapeDtypeStruct((tok, width), bf16),
            jax.ShapeDtypeStruct((tok, dim), f32),
            jax.ShapeDtypeStruct((1, width), f32),
            jax.ShapeDtypeStruct((1, dim), f32),
        ],
        compiler_params=params(60),
        cost_estimate=cost(4 * tok * dim * width, tok * (dim * 6 + width * 4) + w_in.size * 4),
        name="hidden_back",
    )(cotangent, slope, w_back, w_in)


def middle_back_kernel(mid_ref, own_ref, peer_ref, g_ref, gain_ref, w_ref, dh_ref, dr_ref, do_ref, sum_ref):
    step = pl.program_id(0)
    unit, inv = standardize(mid_ref[...])
    grad = own_ref[...] + peer_ref[...]
    dh = g_ref[...].astype(f32) + norm_back(unit, inv, gain_ref[...], grad)
    dh_ref[...] = dh
    dr = dh.astype(bf16)
    dr_ref[...] = dr
    do_ref[...] = nt(dr, w_ref[...]).astype(bf16)

    @pl.when(step == 0)
    def _():
        sum_ref[...] = jnp.zeros_like(sum_ref)

    sum_ref[0:1] += jnp.sum(grad * unit, 0, keepdims=True)
    sum_ref[1:2] += jnp.sum(grad, 0, keepdims=True)
    sum_ref[2:3] += jnp.sum(dr.astype(f32), 0, keepdims=True)


def middle_back(middle, own, peer, cotangent, gain, w_out):
    tok, dim = middle.shape
    width = w_out.shape[0]
    rows = lambda n: pl.BlockSpec((TILE, n), lambda i: (i, 0))
    return pl.pallas_call(
        middle_back_kernel,
        grid=(tok // TILE,),
        in_specs=[rows(dim), rows(dim), rows(dim), rows(dim), whole((1, dim)), whole(w_out.shape)],
        out_specs=[rows(dim), rows(dim), rows(width), whole((8, dim))],
        out_shape=[
            jax.ShapeDtypeStruct((tok, dim), f32),
            jax.ShapeDtypeStruct((tok, dim), bf16),
            jax.ShapeDtypeStruct((tok, width), bf16),
            jax.ShapeDtypeStruct((8, dim), f32),
        ],
        compiler_params=params(60),
        cost_estimate=cost(2 * tok * dim * width, tok * (dim * 20 + width * 2) + w_out.size * 2),
        name="middle_back",
    )(middle, own, peer, cotangent, gain, w_out)


def attend_back_tile(tile, keys, values, rows, grads, mask, lse_rows):
    first = lax.broadcasted_iota(jnp.int32, (1, PAIR), 1) < HEAD_DIM
    zero = jnp.zeros((), bf16)
    parts = []
    for head in range(2):
        pick = lambda a: jnp.where(first, a, zero) if head == 0 else jnp.where(first, zero, a)
        probs = jnp.exp(nt(keys, pick(rows)) + mask - lse_rows[head])
        back = nt(values, pick(grads))
        inner = jnp.sum(probs * back, 0, keepdims=True)
        slant = (probs * (back - inner)).astype(bf16)
        dv = nn(probs.astype(bf16), grads)
        dk = nn(slant, rows)
        dq = tn(slant, keys)
        parts.append((dq, dk, dv))
    dq, dk, dv = (jnp.where(first, a, b) for a, b in zip(*parts))
    return (dq * HEAD_DIM ** (-0.5)).astype(bf16), dk, dv


def attend_back_pair(q, k, v, do, lse, col_ref, row_ref, put_dq, acc_k, acc_v, after=lambda tile: None):
    total = None
    for tile, (start, count, low, high) in enumerate(TILES):
        span = slice(start, start + count)
        mask = jnp.where(col_ref[low:high, 0:1] == row_ref[:, span], 0.0, -1000000000.0)
        dq, dk, dv = attend_back_tile(
            tile, k(slice(low, high)), v(slice(low, high)), q(span), do(span), mask, lse(tile, count)
        )
        put_dq(span, dq)
        top = jnp.sum(dq.astype(f32), 0, keepdims=True)
        total = top if total is None else total + top
        edge = 0 if tile == 0 else TILES[tile - 1][3]
        for acc, part in ((acc_k, dk), (acc_v, dv)):
            if edge > low:
                acc[low:edge, :] += part[: edge - low]
            if edge < high:
                acc[edge:high, :] = part[max(edge - low, 0) :]
        after(tile)
    return total


def attend_back_kernel(q_ref, k_ref, v_ref, do_ref, lse_a, lse_b, col_ref, row_ref, dq_ref, dk_ref, dv_ref, sum_ref, acc_k, acc_v):
    step = pl.program_id(0)

    def lse(tile, count):
        ref = lse_a if tile < 2 else lse_b
        return [ref[tile % 2, pl.ds(2 * step + head, 1), 0:count] for head in range(2)]

    def put_dq(span, value):
        dq_ref[span, :] = value

    take = lambda ref: lambda span: ref[span, :]
    total = attend_back_pair(
        take(q_ref), take(k_ref), take(v_ref), take(do_ref), lse, col_ref, row_ref, put_dq, acc_k, acc_v
    )
    dk_ref[...] = acc_k[...].astype(bf16)
    dv = acc_v[...].astype(bf16)
    dv_ref[...] = dv
    sum_ref[...] = jnp.zeros_like(sum_ref)
    sum_ref[0:1, :] = total
    sum_ref[1:2, :] = jnp.sum(dv.astype(f32), 0, keepdims=True)


def attend_back(q, k, v, do, lse_a, lse_b, ids_col, ids_row):
    tok, width = q.shape
    pair = pl.BlockSpec((tok, PAIR), lambda p: (0, p))
    out = jax.ShapeDtypeStruct((tok, width), bf16)
    return pl.pallas_call(
        attend_back_kernel,
        grid=(width // PAIR,),
        in_specs=[pair, pair, pair, pair, whole(lse_a.shape), whole(lse_b.shape), whole((tok, 1)), whole((1, tok))],
        out_specs=[pair, pair, pair, pl.BlockSpec((8, PAIR), lambda p: (0, p))],
        out_shape=[out, out, out, jax.ShapeDtypeStruct((8, width), f32)],
        scratch_shapes=[pltpu.VMEM((tok, PAIR), f32), pltpu.VMEM((tok, PAIR), f32)],
        compiler_params=params(60),
        cost_estimate=cost(4 * 10 * tok * HALF * width, tok * width * 18),
        name="attend_back",
    )(q, k, v, do, lse_a, lse_b, ids_col, ids_row)


def normed_back_kernel(dq_ref, dk_ref, dv_ref, w_ref, o_ref):
    o_ref[...] = nt(dq_ref[...], w_ref[0]) + nt(dk_ref[...], w_ref[1]) + nt(dv_ref[...], w_ref[2])


def normed_back(dq, dk, dv, w3):
    tok, width = dq.shape
    dim = w3.shape[1]
    rows = lambda n: pl.BlockSpec((TILE, n), lambda i: (i, 0))
    return pl.pallas_call(
        normed_back_kernel,
        grid=(tok // TILE,),
        in_specs=[rows(width), rows(width), rows(width), whole(w3.shape)],
        out_specs=rows(dim),
        out_shape=jax.ShapeDtypeStruct((tok, dim), f32),
        compiler_params=params(60),
        cost_estimate=cost(6 * tok * dim * width, tok * (dim * 4 + width * 6) + w3.size * 2),
        name="normed_back",
    )(dq, dk, dv, w3)


def input_back_kernel(x_ref, own_ref, peer_ref, dh_ref, gain_ref, o_ref, sum_ref):
    step = pl.program_id(0)
    unit, inv = standardize(x_ref[...].astype(f32))
    grad = own_ref[...] + peer_ref[...]
    o_ref[...] = (dh_ref[...] + norm_back(unit, inv, gain_ref[...], grad)).astype(bf16)

    @pl.when(step == 0)
    def _():
        sum_ref[...] = jnp.zeros_like(sum_ref)

    sum_ref[0:1] += jnp.sum(grad * unit, 0, keepdims=True)
    sum_ref[1:2] += jnp.sum(grad, 0, keepdims=True)


def input_back(tokens, own, peer, dh, gain):
    tok, dim = tokens.shape
    rows = pl.BlockSpec((TILE, dim), lambda i: (i, 0))
    return pl.pallas_call(
        input_back_kernel,
        grid=(tok // TILE,),
        in_specs=[rows, rows, rows, rows, whole((1, dim))],
        out_specs=[rows, whole((8, dim))],
        out_shape=[jax.ShapeDtypeStruct((tok, dim), bf16), jax.ShapeDtypeStruct((8, dim), f32)],
        compiler_params=params(60),
        cost_estimate=cost(20 * tok * dim, tok * dim * 16),
        name="input_back",
    )(tokens, own, peer, dh, gain)


def grad_kernel(parts, group, place_ref, a_ref, b_ref, *refs):
    outs, turned = refs[:parts], refs[parts]

    @pl.when(pl.program_id(0) == 0)
    def _():
        flat = jnp.transpose(a_ref[...])
        if group:
            for g in range(flat.shape[0] // group):
                at = pl.multiple_of(place_ref[g] * group, group)
                turned[pl.ds(at, group), :] = flat[g * group : (g + 1) * group, :]
        else:
            turned[...] = flat

    total = nn(turned[...], b_ref[...])
    rows = total.shape[0] // parts
    for i, out in enumerate(outs):
        out[...] = total[i * rows : (i + 1) * rows, :]


def weight_grad(parts, place, a, b):
    tok, dim = a.shape
    width = b.shape[1]
    step = 384
    count = place.shape[0]
    group = dim // count
    if group % 16:
        order = jnp.argsort(place)
        rows = (order[:, None] * group + jnp.arange(group)[None, :]).reshape(dim)
        a = jnp.take(a, rows, axis=1)
        group = 0
    rows = dim // parts
    return pl.pallas_call(
        functools.partial(grad_kernel, parts, group),
        grid_spec=pltpu.PrefetchScalarGridSpec(
            num_scalar_prefetch=1,
            grid=(width // step,),
            in_specs=[
                pl.BlockSpec((tok, dim), lambda i, *_: (0, 0)),
                pl.BlockSpec((tok, step), lambda i, *_: (0, i)),
            ],
            out_specs=[pl.BlockSpec((rows, step), lambda i, *_: (0, i))] * parts,
            scratch_shapes=[pltpu.VMEM((dim, tok), bf16)],
        ),
        out_shape=[jax.ShapeDtypeStruct((rows, width), f32)] * parts,
        compiler_params=params(60),
        cost_estimate=cost(2 * tok * dim * width, tok * (dim + width) * 2 + dim * width * 4),
        name="weight_grad",
    )(place, a, b)


class Exchange:
    def __init__(self, batch):
        side = 1
        while side * side * 4 < batch:
            side *= 2
        self.batch = batch
        sizes = (batch // (side * side), side, side)
        strides = (side * side, side, 1)
        axes = list(zip(sizes, strides))
        slow, mid, fast = axes
        self.orders = ((fast, mid, slow), (mid, fast, slow))
        me = lax.axis_index("batch")
        core = lax.axis_index("tp")
        away = jnp.arange(batch, dtype=jnp.int32) ^ me
        places = []
        for order in self.orders:
            place = jnp.zeros_like(away)
            for size, stride in order:
                place = place * size + (away // stride) % size
            places.append(place)
        self.place = jnp.where(core == 0, places[0], places[1]).astype(jnp.int32)

    def first_parts(self):
        return self.orders[0][0][0]

    def swap(self, block, phase, k):
        perm = []
        for i in range(self.batch):
            for core in range(2):
                _, stride = self.orders[core][phase]
                perm.append((2 * i + core, 2 * (i ^ (k * stride)) + core))
        return lax.ppermute(block, ("batch", "tp"), perm)

    def reduce(self, parts):
        for phase in range(3):
            got = [self.swap(parts[k], phase, k) for k in range(1, len(parts))]
            if phase == 2:
                total = parts[0]
                for g in got:
                    total = total + g
                return total
            size = self.orders[0][phase + 1][0]
            rows = parts[0].shape[0] // size
            cut = lambda a, i: lax.slice_in_dim(a, i * rows, (i + 1) * rows, axis=0)
            following = []
            for i in range(size):
                total = cut(parts[0], i)
                for g in got:
                    total = total + cut(g, i)
                following.append(total)
            parts = following


def other_core(values):
    return lax.ppermute(values, "tp", [(0, 1), (1, 0)])


COUNT = 12
STEPS = 4
PLAN = (
    (), (), (), (), ((0, 0),), (), (), (), ((1, 0),), ((0, 1),), ((2, 0),), (), (), (), (), ((1, 1), (3, 0),), (),
    (), ((5, 0), (3, 1), (4, 0), (0, 2),), ((1, 2),), ((4, 1),), ((6, 0), (2, 1),), ((8, 0),), ((3, 2),), (),
    ((0, 3), (6, 1), (7, 0),), ((1, 3),), ((2, 2),), (), ((4, 2),), (), ((5, 1), (3, 3), (7, 1), (6, 2),),
    ((8, 1),), (), (), ((5, 2),), (), (), ((8, 2),), ((9, 0),), (), (), ((11, 0),),
    ((2, 3), (4, 3), (9, 1), (10, 0), (7, 2), (6, 3), (5, 3), (11, 1), (10, 1), (8, 3), (11, 2), (9, 2), (7, 3), (10, 2), (11, 3), (9, 3), (10, 3),),
)


class Route:
    def __init__(self):
        self.me = lax.axis_index("batch")
        self.core = lax.axis_index("tp")
        self.bits = {s: lax.rem(self.me // s, 2) for s in (1, 2, 4, 8)}
        near = {s: self.me + s * (1 - 2 * self.bits[s]) for s in (1, 2, 4, 8)}
        core = self.core
        side = near[1] * (1 - core) + near[2] * core
        other = near[2] * (1 - core) + near[1] * core
        self.plain = (side, other, near[4], near[8])
        self.turned = (near[4], side, other, near[8])
        self.plain_weight = {1: 8 - 4 * core, 2: 4 + 4 * core, 4: 2, 8: 1}
        self.turned_weight = {4: 8, 1: 4 - 2 * core, 2: 2 + 2 * core, 8: 1}

    def kind(self, chunk):
        return lax.rem(chunk, 3) // 2

    def partner(self, chunk, step):
        kind = self.kind(chunk)
        return self.plain[step] + kind * (self.turned[step] - self.plain[step])

    def places(self, chunk):
        kind = self.kind(chunk)
        terms = {}
        for s in (1, 2, 4, 8):
            weight = self.plain_weight[s] + kind * (self.turned_weight[s] - self.plain_weight[s])
            terms[s] = (self.bits[s] * weight, (1 - self.bits[s]) * weight)
        return [sum(terms[s][(g // s) % 2] for s in (1, 2, 4, 8)) for g in range(16)]


def attend_pair(rows_at, rows, keys, values, mask_ref, put):
    first = lax.broadcasted_iota(jnp.int32, (1, PAIR), 1) < HEAD_DIM
    zero = jnp.zeros((), bf16)
    with_ones = jnp.concatenate([values, jnp.ones_like(values)], 1)
    for at, count in ROWS:
        part = rows(at, count)
        both = jnp.concatenate([jnp.where(first, part, zero), jnp.where(first, zero, part)], 0)
        mask = mask_ref[at : at + count, :]
        scores = nt(both, keys) + jnp.concatenate([mask, mask], 0)
        top = jnp.max(scores, -1, keepdims=True)
        mixed = nn(jnp.exp(scores - top).astype(bf16), with_ones)
        total = mixed[:, PAIR:]
        mixed = mixed[:, :PAIR] / total
        logs = top + jnp.log(total)
        put(at, count, jnp.where(first, mixed[:count], mixed[count:]).astype(bf16), logs[:count], logs[count:])


def layer_kernel(
    tok_h, g_h, w3_h, wo_h, wi_h, wb_h,
    ids_ref, gain1_ref, shift1_ref, qvb_ref, ob_ref, gain2_ref, shift2_ref, ib_ref, bb_ref,
    layer_h, input_h, grads_h, sums_ref, heads_h, hid_h, mid_h,
    buf_h, buf_d, buf_n, buf_g, buf_m, own, peer, wi, wb, wo, acc_k, acc_v, col_ref, query_ids, key_ids, mask_ref,
    bias_ref, lse_ref, chunks, recv0, recv1, recv2, recv3, sums_in,
    load_sem, send_sem, recv_sem, grad_sem, swap_send, swap_recv, sums_send, sums_recv, put_sem, free_sem,
):
    mesh_id = pl.DeviceIdType.MESH
    route = Route()
    me, core = route.me, route.core
    tok, dim = buf_g.shape
    width = buf_h.shape[1]
    third = wo.shape[0]
    tiles = tok // TILE
    blocks = width // LANES
    recvs = (recv0, recv1, recv2, recv3)
    vector = lambda ref: ref[...].reshape(1, -1)

    barrier = pltpu.get_barrier_semaphore()
    for other in route.plain:
        pl.semaphore_signal(barrier, inc=1, device_id=(other, core), device_id_type=mesh_id)
    pl.semaphore_signal(barrier, inc=1, device_id=(me, 1 - core), device_id_type=mesh_id)

    def load(source, target, at):
        copy = pltpu.make_async_copy(source, target, load_sem.at[at])
        copy.start()
        return copy

    def load_w3(at):
        return [load(w3_h.at[c], wi.at[:, pl.ds(c * third, third)], at + c) for c in range(3)]

    tok_load = load(tok_h, buf_d.at[:, pl.ds(0, dim)], 0)
    w3_load = load_w3(1)
    wo_load = load(wo_h, wo, 4)
    g_load = load(g_h, buf_g, 5)
    wb_load = load(wb_h, wb, 7)


    def hop(chunk, step):
        half = 8 >> step
        return pltpu.make_async_remote_copy(
            src_ref=chunks.at[chunk, pl.ds(half, half)],
            dst_ref=recvs[step].at[chunk],
            send_sem=send_sem.at[step, chunk],
            recv_sem=recv_sem.at[step, chunk],
            device_id=(route.partner(chunk, step), core),
            device_id_type=mesh_id,
        )

    def deliver(chunk):
        return pltpu.make_async_copy(chunks.at[chunk, 0], grads_h.at[chunk], grad_sem.at[chunk])

    def finish(chunk, step):
        got = hop(chunk, step)
        got.wait_send()
        got.wait_recv()

        def add(g, carry):
            chunks[chunk, g] += recvs[step][chunk, g]
            return carry

        lax.fori_loop(0, 8 >> step, add, 0)
        if step < STEPS - 1:
            hop(chunk, step + 1).start()
        else:
            deliver(chunk).start()

    left = list(PLAN)

    def arrivals():
        for chunk, step in left.pop(0):
            finish(chunk, step)

    def loop(count, body, planned=True):
        each = [left.pop(0) for _ in range(count)] if planned else []

        def turn(i, carry):
            body(i)
            for at, now in enumerate(each):
                if now:

                    @pl.when(i == at)
                    def _():
                        for chunk, step in now:
                            finish(chunk, step)

            return carry

        lax.fori_loop(0, count, turn, 0)

    def gradient(chunk, source, right):
        places = route.places(chunk)
        total = tn(source[...], right)
        rows = dim // 16
        for g in range(16):
            chunks[chunk, places[g]] = total[g * rows : (g + 1) * rows, :]
        hop(chunk, 0).start()

    def columns(at):
        return pl.ds(pl.multiple_of(at, PAIR), LANES)

    def rows_of(i):
        return pl.ds(pl.multiple_of(i * TILE, TILE), TILE)


    def swap(turn_at, i, rows):
        return pltpu.make_async_remote_copy(
            src_ref=own.at[rows],
            dst_ref=peer.at[rows],
            send_sem=swap_send.at[turn_at, i],
            recv_sem=swap_recv.at[turn_at, i],
            device_id=(me, 1 - core),
            device_id_type=mesh_id,
        )

    def swapped(turn_at, i):
        got = swap(turn_at, i, rows_of(i))
        got.wait_send()
        got.wait_recv()
        return own[rows_of(i), :] + peer[rows_of(i), :]

    def peer_is_free():
        pl.semaphore_signal(free_sem, inc=1, device_id=(me, 1 - core), device_id_type=mesh_id)


    ids = vector(ids_ref)
    for half in range(2):
        query_ids[half, :, 0:HALF] = ids[:, half * HALF : (half + 1) * HALF]
        key_ids[half] = ids[:, half * LOW : half * LOW + WINDOW]
    col_ref[...] = jnp.transpose(jnp.broadcast_to(ids, (PAIR, tok)))
    for c in range(blocks):
        bias_ref[c] = vector(ib_ref)[:, c * LANES : (c + 1) * LANES]
    sums_ref[...] = jnp.zeros_like(sums_ref)
    tok_load.wait()
    for item in w3_load:
        item.wait()

    def first_norm(values):
        unit, inv = standardize(values.astype(f32))
        return unit, inv, (unit * vector(gain1_ref) + vector(shift1_ref)).astype(bf16)

    def body(i):
        _, _, normed = first_norm(buf_d[rows_of(i), 0:dim])
        out = nn(normed, wi[:, 0 : 3 * third])
        query = (out[:, 0:third] + qvb_ref[0:1, :]).astype(bf16)
        buf_h[rows_of(i), 0:third] = (query.astype(f32) * HEAD_DIM ** (-0.5)).astype(bf16)
        buf_h[rows_of(i), third : 2 * third] = out[:, third : 2 * third].astype(bf16)
        buf_h[rows_of(i), 2 * third : 3 * third] = (out[:, 2 * third :] + qvb_ref[1:2, :]).astype(bf16)

    loop(tiles, body, False)
    wi_load = load(wi_h, wi, 6)
    save_qkv = load(buf_h.at[:, pl.ds(0, 3 * third)], heads_h.at[:, pl.ds(0, 3 * third)], 8)


    wo_load.wait()

    def body(half):
        start = pl.multiple_of(half * HALF, TILE)
        window = pl.ds(pl.multiple_of(half * LOW, 64), WINDOW)
        mask_ref[...] = jnp.where(col_ref[pl.ds(start, HALF), 0:1] == key_ids[half], 0.0, -1000000000.0)

        def pair(p):
            pick = lambda block: pl.ds(pl.multiple_of(block * third + p * PAIR, PAIR), PAIR)

            def rows(at, count):
                return buf_h[pl.ds(pl.multiple_of(start + at, 32), count), pick(0)]

            def put(at, count, mixed, *logs):
                buf_h[pl.ds(pl.multiple_of(start + at, 32), count), pick(3)] = mixed
                for head in range(2):
                    lse_ref[half, 2 * p + head, 0:1, at : at + count] = jnp.transpose(logs[head])[0:1, :]

            attend_pair(start, rows, buf_h[window, pick(1)], buf_h[window, pick(2)], mask_ref, put)

        loop(third // PAIR, pair, False)

        @pl.when(half == 0)
        def _():
            pl.semaphore_wait(barrier, STEPS + 1)

        def project(j):
            i = half * (tiles // 2) + j
            own[rows_of(i), :] = nn(buf_h[rows_of(i), 3 * third : 4 * third], wo[...])
            swap(0, i, rows_of(i)).start()

        loop(tiles // 2, project, False)

    loop(2, body, False)
    save_o = load(buf_h.at[:, pl.ds(3 * third, third)], heads_h.at[:, pl.ds(3 * third, third)], 9)


    wi_load.wait()
    save_qkv.wait()
    root = 0.7978845608028654

    def hidden(i, c):
        u = nn(buf_n[rows_of(i), :], wi[:, columns(c * LANES)]) + bias_ref[c]
        t = jnp.tanh(u * (root + (root * 0.044715) * (u * u)))
        buf_h[rows_of(i), columns(c * LANES)] = (u * (0.5 + 0.5 * t)).astype(bf16)
        buf_d[rows_of(i), columns(c * LANES)] = u.astype(bf16)

    def body(i):
        total = swapped(0, i)
        middle = buf_d[rows_of(i), 0:dim].astype(f32) + total + vector(ob_ref)
        buf_m[rows_of(i), :] = middle
        unit, _ = standardize(middle)
        buf_n[rows_of(i), :] = (unit * vector(gain2_ref) + vector(shift2_ref)).astype(bf16)
        hidden(i, 0)

    loop(tiles, body, False)
    peer_is_free()
    save_mid = load(buf_m, mid_h, 10)
    save_o.wait()
    g_load.wait()
    gradient(0, buf_g, buf_h[:, 0:LANES])
    arrivals()

    def body(j):
        c = j + 1
        loop(tiles, lambda i: hidden(i, c), False)
        gradient(c, buf_g, buf_h[:, columns(c * LANES)])

    loop(blocks - 1, body)
    save_hid = load(buf_h, hid_h, 11)


    wb_load.wait()
    pl.semaphore_wait(free_sem, 1)

    def body(i):
        grad = buf_g[rows_of(i), :]
        for at in range(0, width, 512):
            u = buf_d[rows_of(i), at : at + 512].astype(f32)
            square = u * u
            t = jnp.tanh(u * (root + (root * 0.044715) * square))
            slope = 0.5 + 0.5 * t + (0.5 * u) * (1.0 - t * t) * (root + (3.0 * 0.044715 * root) * square)
            du = (nt(grad, wb[at : at + 512, :]) * slope).astype(bf16)
            buf_d[rows_of(i), at : at + 512] = du
            sums_ref[4:5, at : at + 512] += jnp.sum(du.astype(f32), 0, keepdims=True)
        own[rows_of(i), :] = nt(buf_d[rows_of(i), :], wi[...])
        swap(1, i, rows_of(i)).start()
        sums_ref[2:3, dim : 2 * dim] += jnp.sum(grad.astype(f32), 0, keepdims=True)

    loop(tiles, body)
    w3_late = load_w3(1)
    save_hid.wait()
    heads_load = load(heads_h, buf_h, 8)


    loop(4, lambda i: gradient(4 + i, buf_n, buf_d[:, columns(i * LANES)]))


    save_mid.wait()

    def body(i):
        grad = swapped(1, i)
        unit, inv = standardize(buf_m[rows_of(i), :])
        dh = buf_g[rows_of(i), :].astype(f32) + norm_back(unit, inv, vector(gain2_ref), grad)
        buf_m[rows_of(i), :] = dh
        dr = dh.astype(bf16)
        buf_n[rows_of(i), :] = dr
        buf_d[rows_of(i), 0:third] = nt(dr, wo[...]).astype(bf16)
        sums_ref[1:2, dim : 2 * dim] += jnp.sum(grad * unit, 0, keepdims=True)
        sums_ref[2:3, 0:dim] += jnp.sum(grad, 0, keepdims=True)
        sums_ref[1:2, 0:dim] += jnp.sum(dr.astype(f32), 0, keepdims=True)

    loop(tiles, body)
    peer_is_free()
    tok_late = load(tok_h, buf_g, 0)
    heads_load.wait()
    gradient(8, buf_n, buf_h[:, 3 * third : 4 * third])
    arrivals()


    first = lax.broadcasted_iota(jnp.int32, (1, PAIR), 1) < HEAD_DIM
    zero = jnp.zeros((), bf16)

    def body(at):
        p, half = at // 2, lax.rem(at, 2)
        pick = lambda block: pl.ds(pl.multiple_of(block * third + p * PAIR, PAIR), PAIR)
        window = pl.ds(pl.multiple_of(half * LOW, 64), WINDOW)
        keys, values = buf_h[window, pick(1)], buf_h[window, pick(2)]

        @pl.when(half == 0)
        def _():
            acc_k[...] = jnp.zeros_like(acc_k)
            acc_v[...] = jnp.zeros_like(acc_v)

        for begin, count in ((0, 256), (256, 352)):
            span = pl.ds(pl.multiple_of(half * HALF + begin, 32), count)
            rows, grads = buf_h[span, pick(0)], buf_d[span, pick(0)]
            same = col_ref[window, 0:1] == query_ids[half, :, begin : begin + count]
            mask = jnp.where(same, 0.0, -1000000000.0)
            parts = []
            for head in range(2):
                own_part = lambda a: jnp.where(first, a, zero) if head == 0 else jnp.where(first, zero, a)
                lse = lse_ref[half, 2 * p + head, 0:1, begin : begin + count]
                probs = jnp.exp(nt(keys, own_part(rows)) + mask - lse)
                back = nt(values, own_part(grads))
                inner = jnp.sum(probs * back, 0, keepdims=True)
                slant = (probs * (back - inner)).astype(bf16)
                parts.append((tn(slant, keys), nn(slant, rows), nn(probs.astype(bf16), grads)))
            dq, dk, dv = (jnp.where(first, a, b) for a, b in zip(*parts))
            dq = (dq * HEAD_DIM ** (-0.5)).astype(bf16)
            buf_d[span, pick(1)] = dq
            sums_ref[3:4, pick(0)] += jnp.sum(dq.astype(f32), 0, keepdims=True)
            acc_k[window, :] += dk
            acc_v[window, :] += dv

        @pl.when(half == 1)
        def _():
            buf_d[:, pick(2)] = acc_k[...].astype(bf16)
            dv = acc_v[...].astype(bf16)
            buf_d[:, pick(3)] = dv
            sums_ref[3:4, pick(1)] = jnp.sum(dv.astype(f32), 0, keepdims=True)

    loop(2 * (third // PAIR), body)
    hid_load = load(hid_h, buf_h, 8)


    tok_late.wait()

    def body(i):
        _, _, normed = first_norm(buf_g[rows_of(i), :])
        buf_n[rows_of(i), :] = normed

    loop(tiles, body, False)
    arrivals()
    loop(3, lambda i: gradient(9 + i, buf_n, buf_d[:, columns(third + i * LANES)]))


    for item in w3_late:
        item.wait()
    pl.semaphore_wait(free_sem, 1)

    def body(i):
        own[rows_of(i), :] = nt(buf_d[rows_of(i), third : 4 * third], wi[:, 0 : 3 * third])
        swap(2, i, rows_of(i)).start()

    loop(tiles, body)

    def body(i):
        grad = swapped(2, i)
        unit, inv, _ = first_norm(buf_g[rows_of(i), :])
        buf_g[rows_of(i), :] = (buf_m[rows_of(i), :] + norm_back(unit, inv, vector(gain1_ref), grad)).astype(bf16)
        sums_ref[0:1, 0:dim] += jnp.sum(grad * unit, 0, keepdims=True)
        sums_ref[0:1, dim : 2 * dim] += jnp.sum(grad, 0, keepdims=True)

    loop(tiles, body)
    peer_is_free()
    input_put = pltpu.make_async_copy(buf_g, input_h, put_sem.at[1])
    input_put.start()
    mid_load = load(mid_h, buf_m, 10)

    def whole_hop(step):
        return pltpu.make_async_remote_copy(
            src_ref=sums_ref,
            dst_ref=sums_in.at[step],
            send_sem=sums_send.at[step],
            recv_sem=sums_recv.at[step],
            device_id=(route.plain[step], core),
            device_id_type=mesh_id,
        )

    def add_sums(step):
        whole_hop(step).wait()
        sums_ref[...] += sums_in[step]

    whole_hop(0).start()


    hid_load.wait()
    pl.semaphore_wait(free_sem, 1)

    def body(i):
        own[rows_of(i), :] = nn(buf_h[rows_of(i), :], wb[...])
        swap(3, i, rows_of(i)).start()

    loop(tiles, body)
    add_sums(0)
    whole_hop(1).start()
    mid_load.wait()

    def body(i):
        buf_n[rows_of(i), :] = (buf_m[rows_of(i), :] + swapped(3, i) + vector(bb_ref)).astype(bf16)

    loop(tiles, body)
    layer_put = pltpu.make_async_copy(buf_n, layer_h, put_sem.at[0])
    layer_put.start()
    rest = left.pop(0)
    gap = len(rest) // STEPS
    for step in range(1, STEPS):
        for item in rest[(step - 1) * gap : step * gap]:
            finish(*item)
        add_sums(step)
        if step + 1 < STEPS:
            whole_hop(step + 1).start()
    for item in rest[(STEPS - 1) * gap :]:
        finish(*item)
    for chunk in range(COUNT):
        deliver(chunk).wait()
    input_put.wait()
    layer_put.wait()


def whole_layer(tokens, g, w3, wo, wi, wb, ids, gain1, shift1, qvb, ob, gain2, shift2, ib, bb):
    tok, dim = g.shape
    width = wi.shape[1]
    third = wo.shape[0]
    rows = dim // 16
    hbm = pl.BlockSpec(memory_space=pl.ANY)
    vmem = pl.BlockSpec(memory_space=pltpu.VMEM)
    dma = pltpu.SemaphoreType.DMA
    return pl.pallas_call(
        layer_kernel,
        in_specs=[hbm] * 6 + [vmem] * 9,
        out_specs=[hbm, hbm, hbm, vmem, hbm, hbm, hbm],
        out_shape=[
            jax.ShapeDtypeStruct((tok, dim), bf16),
            jax.ShapeDtypeStruct((tok, dim), bf16),
            jax.ShapeDtypeStruct((COUNT, rows, LANES), f32),
            jax.ShapeDtypeStruct((8, width), f32),
            jax.ShapeDtypeStruct((tok, width), bf16),
            jax.ShapeDtypeStruct((tok, width), bf16),
            jax.ShapeDtypeStruct((tok, dim), f32),
        ],
        scratch_shapes=[
            pltpu.VMEM((tok, width), bf16),
            pltpu.VMEM((tok, width), bf16),
            pltpu.VMEM((tok, dim), bf16),
            pltpu.VMEM((tok, dim), bf16),
            pltpu.VMEM((tok, dim), f32),
            pltpu.VMEM((tok, dim), f32),
            pltpu.VMEM((tok, dim), f32),
            pltpu.VMEM((dim, width), bf16),
            pltpu.VMEM((width, dim), bf16),
            pltpu.VMEM((third, dim), bf16),
            pltpu.VMEM((tok, PAIR), f32),
            pltpu.VMEM((tok, PAIR), f32),
            pltpu.VMEM((tok, PAIR), jnp.int32),
            pltpu.VMEM((2, 1, 640), jnp.int32),
            pltpu.VMEM((2, 1, WINDOW), jnp.int32),
            pltpu.VMEM((HALF, WINDOW), f32),
            pltpu.VMEM((width // LANES, 1, LANES), f32),
            pltpu.VMEM((2, third // HEAD_DIM, 8, 640), f32),
            pltpu.VMEM((COUNT, 16, rows, LANES), f32),
            pltpu.VMEM((COUNT, 8, rows, LANES), f32),
            pltpu.VMEM((COUNT, 4, rows, LANES), f32),
            pltpu.VMEM((COUNT, 2, rows, LANES), f32),
            pltpu.VMEM((COUNT, 1, rows, LANES), f32),
            pltpu.VMEM((STEPS, 8, width), f32),
            dma((12,)),
            dma((STEPS, COUNT)),
            dma((STEPS, COUNT)),
            dma((COUNT,)),
            dma((4, tok // TILE)),
            dma((4, tok // TILE)),
            dma((STEPS,)),
            dma((STEPS,)),
            dma((2,)),
            pltpu.SemaphoreType.REGULAR,
        ],
        compiler_params=pltpu.CompilerParams(vmem_limit_bytes=VMEM_LIMIT, collective_id=0, has_side_effects=True),
        cost_estimate=cost(34e9, 40e6),
        name="whole_layer",
    )(tokens, g, w3, wo, wi, wb, ids, gain1, shift1, qvb, ob, gain2, shift2, ib, bb)


def outputs_kernel(layer_h, input_h, grads_h, sums_ref, layer_o, input_o, *refs):
    n1g, n1s, qkv, qvb, out, obg, n2g, n2s, inw, ibg, back, bbg, held, kept, in_sem, out_sem = refs
    me = lax.axis_index("batch")
    dim = sums_ref.shape[1] // 2
    third = dim // 2
    pieces = 4
    rows = held.shape[1] // pieces
    grads_in = pltpu.make_async_copy(grads_h, kept, in_sem.at[2 * pieces])
    grads_in.start()
    moves = []
    for i, (source, target) in enumerate(((layer_h, layer_o), (input_h, input_o))):
        for j in range(pieces):
            span = pl.ds(j * rows, rows)
            at = i * pieces + j
            coming = pltpu.make_async_copy(source.at[span], held.at[i, span], in_sem.at[at])
            coming.start()
            moves.append((coming, pltpu.make_async_copy(held.at[i, span], target.at[span], out_sem.at[at])))

    def mine(row, at, size):
        n = size // 16
        values = jnp.broadcast_to(sums_ref[row : row + 1, at : at + size], (8, size))
        return pltpu.roll(values, size - me * n, 1)[0:1, 0:n]

    for ref, row, at in ((n1g, 0, 0), (n1s, 0, dim), (obg, 1, 0), (n2g, 1, dim), (n2s, 2, 0), (bbg, 2, dim)):
        ref[...] = mine(row, at, dim).reshape(-1)
    ibg[...] = mine(4, 0, 2 * dim).reshape(-1)
    qvb[0:1, :] = mine(3, 0, third)
    qvb[1:2, :] = mine(3, third, third)
    grads_in.wait()
    places = [back.at[:, pl.ds(c * LANES, LANES)] for c in range(4)]
    places += [inw.at[:, pl.ds(c * LANES, LANES)] for c in range(4)]
    places += [out] + [qkv.at[c] for c in range(3)]
    going = [pltpu.make_async_copy(kept.at[c], place, out_sem.at[2 * pieces + c]) for c, place in enumerate(places)]
    for item in going:
        item.start()
    for coming, leaving in moves:
        coming.wait()
        leaving.start()
    for item in going:
        item.wait()
    for _, leaving in moves:
        leaving.wait()


def outputs(layer, grad, grads, sums):
    rows, width = grads.shape[1], sums.shape[1]
    hbm = pl.BlockSpec(memory_space=pl.ANY)
    vmem = pl.BlockSpec(memory_space=pltpu.VMEM)
    small = jax.ShapeDtypeStruct((rows,), f32)
    shape = lambda *s: jax.ShapeDtypeStruct(s, f32)
    return pl.pallas_call(
        outputs_kernel,
        in_specs=[hbm, hbm, hbm, vmem],
        out_specs=[hbm, hbm, vmem, vmem, hbm, vmem, hbm, vmem, vmem, vmem, hbm, vmem, hbm, vmem],
        out_shape=[
            jax.ShapeDtypeStruct(layer.shape, bf16),
            jax.ShapeDtypeStruct(grad.shape, bf16),
            small,
            small,
            shape(3, rows, LANES),
            shape(2, rows // 2),
            shape(rows, LANES),
            small,
            small,
            small,
            shape(rows, width),
            shape(2 * rows),
            shape(rows, width),
            small,
        ],
        scratch_shapes=[
            pltpu.VMEM((2,) + layer.shape, bf16),
            pltpu.VMEM(grads.shape, f32),
            pltpu.SemaphoreType.DMA((9,)),
            pltpu.SemaphoreType.DMA((8 + COUNT,)),
        ],
        compiler_params=params(60),
        name="outputs",
    )(layer, grad, grads, sums)


def shards(
    tokens,
    seq_ids,
    cotangent,
    norm1_gain,
    norm1_shift,
    w_qkv,
    qv_bias,
    w_out,
    out_bias,
    norm2_gain,
    norm2_shift,
    w_in,
    in_bias,
    w_back,
    back_bias,
    batch,
):
    tok, dim = tokens.shape
    w3 = jnp.transpose(w_qkv, (1, 0, 2))
    if batch == 16:
        layer, grad, grads, sums, *_ = whole_layer(
            tokens, cotangent, w3, w_out, w_in, w_back, seq_ids,
            norm1_gain, norm1_shift, qv_bias, out_bias, norm2_gain, norm2_shift, in_bias, back_bias,
        )
        results = list(outputs(layer, grad, grads, sums))
        results[4] = jnp.transpose(results[4], (1, 0, 2))
        results[6], results[12] = results[6].T, results[12].T
        return tuple(results)

    row = lambda a: a.reshape(1, -1)
    ids_col, ids_row = seq_ids.reshape(tok, 1), seq_ids.reshape(1, tok)
    exchange = Exchange(batch)
    parts = exchange.first_parts()

    normed, q, k, v = project(tokens, row(norm1_gain), row(norm1_shift), w3, qv_bias)
    mixed, lse_a, part_a = attend(0, q, k, v, ids_col, ids_row, w_out)
    peer_a = other_core(part_a)
    mixed, lse_b, part_b = attend(1, q, k, v, ids_col, ids_row, w_out, (mixed,))
    peer_b = other_core(part_b)
    mlp = (row(out_bias), row(norm2_gain), row(norm2_shift), w_in, row(in_bias))
    state = hidden_layer(0, tokens, part_a, peer_a, *mlp)
    state = hidden_layer(1, tokens, part_b, peer_b, *mlp, before=tuple(state))
    middle, normed_two, hidden, slope = state

    back_parts = weight_grad(parts, exchange.place, cotangent, hidden)
    du, dn2, in_bias_sum, back_bias_sum = hidden_back(cotangent, slope, w_back, w_in)
    dn2_peer = other_core(dn2)
    in_parts = weight_grad(parts, exchange.place, normed_two, du)
    mlp_own = rows_matmul(hidden, w_back)
    mlp_peer = other_core(mlp_own)
    dh, dr, do, middle_sums = middle_back(middle, dn2, dn2_peer, cotangent, row(norm2_gain), w_out)
    out_parts = weight_grad(parts, exchange.place, dr, mixed)
    layer_out = (middle + (mlp_own + mlp_peer) + back_bias).astype(bf16)
    dq, dk, dv, qv_sums = attend_back(q, k, v, do, lse_a, lse_b, ids_col, ids_row)
    q_parts = weight_grad(parts, exchange.place, normed, dq)
    k_parts = weight_grad(parts, exchange.place, normed, dk)
    v_parts = weight_grad(parts, exchange.place, normed, dv)
    dn1 = normed_back(dq, dk, dv, w3)
    dn1_peer = other_core(dn1)
    tokens_grad, input_sums = input_back(tokens, dn1, dn1_peer, dh, row(norm1_gain))

    w_back_grad = jnp.transpose(exchange.reduce(back_parts))
    w_in_grad = exchange.reduce(in_parts)
    w_out_grad = jnp.transpose(exchange.reduce(out_parts))
    w_qkv_grad = jnp.stack([exchange.reduce(p) for p in (q_parts, k_parts, v_parts)], 1)

    pieces = [input_sums[0], input_sums[1], middle_sums[2], middle_sums[0], middle_sums[1], back_bias_sum[0]]
    pieces += [qv_sums[0], qv_sums[1], in_bias_sum[0]]
    packed = jnp.concatenate([p.reshape(batch, -1) for p in pieces], 1)
    vectors = lax.psum_scatter(packed, "batch", scatter_dimension=0, tiled=True)[0]
    out, at = [], 0
    for p in pieces:
        n = p.shape[0] // batch
        out.append(vectors[at : at + n])
        at += n
    n1g, n1s, obg, n2g, n2s, bbg, qb, vb, ibg = out
    return (
        layer_out,
        tokens_grad,
        n1g,
        n1s,
        w_qkv_grad,
        jnp.stack([qb, vb]),
        w_out_grad,
        obg,
        n2g,
        n2s,
        w_in_grad,
        ibg,
        w_back_grad,
        bbg,
    )


def solution(mesh):
    in_specs = (
        P("batch", None),
        P("batch"),
        P("batch", None),
        P(),
        P(),
        P(None, None, "tp"),
        P(None, "tp"),
        P("tp", None),
        P(),
        P(),
        P(),
        P(None, "tp"),
        P("tp"),
        P("tp", None),
        P(),
    )
    out_specs = (
        P("batch", None),
        P("batch", None),
        P("batch"),
        P("batch"),
        P("batch", None, "tp"),
        P(None, ("tp", "batch")),
        P("tp", "batch"),
        P("batch"),
        P("batch"),
        P("batch"),
        P("batch", "tp"),
        P(("tp", "batch")),
        P("tp", "batch"),
        P("batch"),
    )
    body = functools.partial(shards, batch=mesh.shape["batch"])
    return jax.shard_map(body, mesh=mesh, in_specs=in_specs, out_specs=out_specs, check_vma=False)
```

profile of v0, /device:TPU:0, one launch (start us, length us, event | category | flops | bytes accessed | tf_op | source)
XLA Modules:
  0.0 159.2 jit_solution(3262240176314628114)
XLA Ops:
  0.7 153.1 %whole_layer.1 = (bf16[1216,768]{1,0:T(8,128)(2,1)}, bf16[1216,768]{1,0:T(8,128)(2,1)}, f32[12,48,384]{2,1,0:T(8,128)}, f32[8,1536]{1,0:T(8,128)}, bf16[1216,153...) custom-call(bf16[1216,768]{1,0:T(8,128)(2,1)} %tok_h.1, bf16[1216,768]{1,0:T(8,128)(2,1)} %g_h.1, ...), custom_call_target="tpu_custom_call" | custom-call | flops 33999998976 | bytes 40000000 | tf_op jit(solution)/shard_map/whole_layer/pallas_call | solution.py:1035
  153.8 5.2 %outputs.1 = (bf16[1216,768]{1,0:T(8,128)(2,1)}, bf16[1216,768]{1,0:T(8,128)(2,1)}, f32[48]{0:T(128)}, f32[48]{0:T(128)}, f32[3,48,384]{2,1,0:T(8,128)}, /*index...) custom-call(bf16[1216,768]{1,0:T(8,128)(2,1)} %get-tuple-element.32., ...), custom_call_target="tpu_custom_call" | custom-call | tf_op jit(solution)/shard_map/outputs/pallas_call | solution.py:1140
where the time goes:
time: 159 us
  Pallas kernels  158 us (99%)
    pallas_call x1, Pallas kernels, whole_layer(): pl.pallas_call(layer_kernel, in_specs=[hbm] * 6 + [vmem] * 9, out_specs=[...  153 us
    pallas_call x1, Pallas kernels, outputs(): pl.pallas_call(outputs_kernel, in_specs=[hbm, hbm, hbm, vmem], out_specs=...  5.2 us

commit v1 on v0

--- a/solution.py
+++ b/solution.py
@@ -571,32 +571,42 @@
 )
 
 
+ORDERS = ((1, 2, 4, 8), (4, 1, 2, 8), (1, 4, 2, 8))
+ORDER_OF = (0, 0, 1, 0, 0, 1, 0, 0, 1, 0, 0, 1)
+
+
 class Route:
     def __init__(self):
         self.me = lax.axis_index("batch")
-        self.core = lax.axis_index("tp")
+        self.core = core = lax.axis_index("tp")
         self.bits = {s: lax.rem(self.me // s, 2) for s in (1, 2, 4, 8)}
         near = {s: self.me + s * (1 - 2 * self.bits[s]) for s in (1, 2, 4, 8)}
-        core = self.core
         side = near[1] * (1 - core) + near[2] * core
         other = near[2] * (1 - core) + near[1] * core
         self.plain = (side, other, near[4], near[8])
-        self.turned = (near[4], side, other, near[8])
-        self.plain_weight = {1: 8 - 4 * core, 2: 4 + 4 * core, 4: 2, 8: 1}
-        self.turned_weight = {4: 8, 1: 4 - 2 * core, 2: 2 + 2 * core, 8: 1}
-
-    def kind(self, chunk):
-        return lax.rem(chunk, 3) // 2
+        self.near = {1: side, 2: other, 4: near[4], 8: near[8]}
+        self.weights = []
+        for order in ORDERS:
+            at = {s: 8 >> order.index(s) for s in order}
+            first, second = at[1] * (1 - core) + at[2] * core, at[2] * (1 - core) + at[1] * core
+            self.weights.append({1: first, 2: second, 4: at[4], 8: at[8]})
+
+    def by_order(self, chunk, values):
+        if isinstance(chunk, int):
+            return values[ORDER_OF[chunk]]
+        total = values[0]
+        for kind in range(1, len(ORDERS)):
+            own = sum((chunk == c).astype(jnp.int32) for c in range(COUNT) if ORDER_OF[c] == kind)
+            total = total + own * (values[kind] - values[0])
+        return total
 
     def partner(self, chunk, step):
-        kind = self.kind(chunk)
-        return self.plain[step] + kind * (self.turned[step] - self.plain[step])
+        return self.by_order(chunk, [self.near[order[step]] for order in ORDERS])
 
     def places(self, chunk):
-        kind = self.kind(chunk)
         terms = {}
         for s in (1, 2, 4, 8):
-            weight = self.plain_weight[s] + kind * (self.turned_weight[s] - self.plain_weight[s])
+            weight = self.by_order(chunk, [w[s] for w in self.weights])
             terms[s] = (self.bits[s] * weight, (1 - self.bits[s]) * weight)
         return [sum(terms[s][(g // s) % 2] for s in (1, 2, 4, 8)) for g in range(16)]
 
@@ -623,7 +633,7 @@
     ids_ref, gain1_ref, shift1_ref, qvb_ref, ob_ref, gain2_ref, shift2_ref, ib_ref, bb_ref,
     layer_h, input_h, grads_h, sums_ref, heads_h, hid_h, mid_h,
     buf_h, buf_d, buf_n, buf_g, buf_m, own, peer, wi, wb, wo, acc_k, acc_v, col_ref, query_ids, key_ids, mask_ref,
-    bias_ref, lse_ref, chunks, recv0, recv1, recv2, recv3, sums_in,
+    bias_ref, lse_ref, log_ref, chunks, recv0, recv1, recv2, recv3, sums_in,
     load_sem, send_sem, recv_sem, grad_sem, swap_send, swap_recv, sums_send, sums_recv, put_sem, free_sem,
 ):
     mesh_id = pl.DeviceIdType.MESH
@@ -653,8 +663,6 @@
     tok_load = load(tok_h, buf_d.at[:, pl.ds(0, dim)], 0)
     w3_load = load_w3(1)
     wo_load = load(wo_h, wo, 4)
-    g_load = load(g_h, buf_g, 5)
-    wb_load = load(wb_h, wb, 7)
 
 
     def hop(chunk, step):
@@ -760,7 +768,7 @@
         unit, inv = standardize(values.astype(f32))
         return unit, inv, (unit * vector(gain1_ref) + vector(shift1_ref)).astype(bf16)
 
-    def body(i):
+    def project_rows(i):
         _, _, normed = first_norm(buf_d[rows_of(i), 0:dim])
         out = nn(normed, wi[:, 0 : 3 * third])
         query = (out[:, 0:third] + qvb_ref[0:1, :]).astype(bf16)
@@ -768,12 +776,20 @@
         buf_h[rows_of(i), third : 2 * third] = out[:, third : 2 * third].astype(bf16)
         buf_h[rows_of(i), 2 * third : 3 * third] = (out[:, 2 * third :] + qvb_ref[1:2, :]).astype(bf16)
 
-    loop(tiles, body, False)
+    def body(i):
+        project_rows(2 * i)
+        project_rows(2 * i + 1)
+
+    loop(tiles // 2, body, False)
     wi_load = load(wi_h, wi, 6)
+    g_load = load(g_h, buf_g, 5)
+    wb_load = load(wb_h, wb, 7)
     save_qkv = load(buf_h.at[:, pl.ds(0, 3 * third)], heads_h.at[:, pl.ds(0, 3 * third)], 8)
 
 
     wo_load.wait()
+    log_ref[...] = jnp.zeros_like(log_ref)
+    lane = lax.broadcasted_iota(jnp.int32, (1, PAIR), 1) // 8
 
     def body(half):
         start = pl.multiple_of(half * HALF, TILE)
@@ -787,13 +803,19 @@
                 return buf_h[pl.ds(pl.multiple_of(start + at, 32), count), pick(0)]
 
             def put(at, count, mixed, *logs):
-                buf_h[pl.ds(pl.multiple_of(start + at, 32), count), pick(3)] = mixed
+                buf_n[pl.ds(pl.multiple_of(start + at, 32), count), pick(0)] = mixed
+                old = log_ref[at : at + count, :]
                 for head in range(2):
-                    lse_ref[half, 2 * p + head, 0:1, at : at + count] = jnp.transpose(logs[head])[0:1, :]
+                    old = jnp.where(lane == 2 * p + head, logs[head], old)
+                log_ref[at : at + count, :] = old
 
             attend_pair(start, rows, buf_h[window, pick(1)], buf_h[window, pick(2)], mask_ref, put)
 
         loop(third // PAIR, pair, False)
+
+        turned = jnp.transpose(log_ref[...])
+        for head in range(third // HEAD_DIM):
+            lse_ref[half, head, 0:1, 0:HALF] = turned[head * 8 : head * 8 + 1, :]
 
         @pl.when(half == 0)
         def _():
@@ -801,17 +823,18 @@
 
         def project(j):
             i = half * (tiles // 2) + j
-            own[rows_of(i), :] = nn(buf_h[rows_of(i), 3 * third : 4 * third], wo[...])
+            own[rows_of(i), :] = nn(buf_n[rows_of(i), 0:third], wo[...])
             swap(0, i, rows_of(i)).start()
 
         loop(tiles // 2, project, False)
 
     loop(2, body, False)
-    save_o = load(buf_h.at[:, pl.ds(3 * third, third)], heads_h.at[:, pl.ds(3 * third, third)], 9)
+    save_o = load(buf_n.at[:, pl.ds(0, third)], heads_h.at[:, pl.ds(3 * third, third)], 9)
 
 
     wi_load.wait()
     save_qkv.wait()
+    save_o.wait()
     root = 0.7978845608028654
 
     def hidden(i, c):
@@ -831,7 +854,6 @@
     loop(tiles, body, False)
     peer_is_free()
     save_mid = load(buf_m, mid_h, 10)
-    save_o.wait()
     g_load.wait()
     gradient(0, buf_g, buf_h[:, 0:LANES])
     arrivals()
@@ -1064,6 +1086,7 @@
             pltpu.VMEM((HALF, WINDOW), f32),
             pltpu.VMEM((width // LANES, 1, LANES), f32),
             pltpu.VMEM((2, third // HEAD_DIM, 8, 640), f32),
+            pltpu.VMEM((HALF, PAIR), f32),
             pltpu.VMEM((COUNT, 16, rows, LANES), f32),
             pltpu.VMEM((COUNT, 8, rows, LANES), f32),
             pltpu.VMEM((COUNT, 4, rows, LANES), f32),

time: 159 us -> 149 us (0.937)
  Pallas kernels: 158 us -> 148 us
    pallas_call x1, Pallas kernels: 153 us -> 143 us  [whole_layer(): pl.pallas_call(layer_kernel, in_specs=[hbm] * 6 + [vmem] * 9, out_specs=[...]
where the time goes in v1:
time: 149 us
  Pallas kernels  148 us (99%)
    pallas_call x1, Pallas kernels, whole_layer(): pl.pallas_call(layer_kernel, in_specs=[hbm] * 6 + [vmem] * 9, out_specs=[...  143 us
    pallas_call x1, Pallas kernels, outputs(): pl.pallas_call(outputs_kernel, in_specs=[hbm, hbm, hbm, vmem], out_specs=...  5.2 us

profile of v1, /device:TPU:0, one launch (start us, length us, event | category | flops | bytes accessed | tf_op | source)
XLA Modules:
  0.0 149.2 jit_solution(16703505630293664627)
XLA Ops:
  0.7 143.2 %whole_layer.1 = (bf16[1216,768]{1,0:T(8,128)(2,1)}, bf16[1216,768]{1,0:T(8,128)(2,1)}, f32[12,48,384]{2,1,0:T(8,128)}, f32[8,1536]{1,0:T(8,128)}, bf16[1216,153...) custom-call(bf16[1216,768]{1,0:T(8,128)(2,1)} %tok_h.1, bf16[1216,768]{1,0:T(8,128)(2,1)} %g_h.1, ...), custom_call_target="tpu_custom_call" | custom-call | flops 33999998976 | bytes 40000000 | tf_op jit(solution)/shard_map/whole_layer/pallas_call | solution.py:1057
  143.9 5.2 %outputs.1 = (bf16[1216,768]{1,0:T(8,128)(2,1)}, bf16[1216,768]{1,0:T(8,128)(2,1)}, f32[48]{0:T(128)}, f32[48]{0:T(128)}, f32[3,48,384]{2,1,0:T(8,128)}, /*index...) custom-call(bf16[1216,768]{1,0:T(8,128)(2,1)} %get-tuple-element.32., ...), custom_call_target="tpu_custom_call" | custom-call | tf_op jit(solution)/shard_map/outputs/pallas_call | solution.py:1163

commit v2 on v1

--- a/solution.py
+++ b/solution.py
@@ -563,11 +563,11 @@
 COUNT = 12
 STEPS = 4
 PLAN = (
-    (), (), (), (), ((0, 0),), (), (), (), ((1, 0),), ((0, 1),), ((2, 0),), (), (), (), (), ((1, 1), (3, 0),), (),
-    (), ((5, 0), (3, 1), (4, 0), (0, 2),), ((1, 2),), ((4, 1),), ((6, 0), (2, 1),), ((8, 0),), ((3, 2),), (),
-    ((0, 3), (6, 1), (7, 0),), ((1, 3),), ((2, 2),), (), ((4, 2),), (), ((5, 1), (3, 3), (7, 1), (6, 2),),
-    ((8, 1),), (), (), ((5, 2),), (), (), ((8, 2),), ((9, 0),), (), (), ((11, 0),),
-    ((2, 3), (4, 3), (9, 1), (10, 0), (7, 2), (6, 3), (5, 3), (11, 1), (10, 1), (8, 3), (11, 2), (9, 2), (7, 3), (10, 2), (11, 3), (9, 3), (10, 3),),
+    (), (), (), (), ((0, 0),), (), (), ((1, 0), (0, 1),), ((2, 0),), (), (), ((0, 2),), (), ((1, 1),), ((3, 0),),
+    (), (), (), ((3, 1), (5, 0), (4, 0), (0, 3),), ((2, 1), (1, 2),), ((4, 1),), ((2, 2), (6, 0),), ((8, 0),),
+    ((3, 2),), ((1, 3), (6, 1),), ((7, 0),), ((4, 2),), (), ((5, 1), (2, 3),), (), ((3, 3),),
+    ((7, 1), (6, 2), (8, 1),), (), ((5, 2),), (), (), ((8, 2),), (), (), ((9, 0),), (), ((11, 0),), (),
+    ((4, 3), (7, 2), (10, 0), (9, 1), (6, 3), (5, 3), (11, 1), (8, 3), (10, 1), (7, 3), (11, 2), (9, 2), (10, 2), (11, 3), (9, 3), (10, 3),),
 )
 
 

time: 149 us -> 149 us (level)
  no operation moved by 1% of the time
where the time goes in v2:
time: 149 us
  Pallas kernels  148 us (99%)
    pallas_call x1, Pallas kernels, whole_layer(): pl.pallas_call(layer_kernel, in_specs=[hbm] * 6 + [vmem] * 9, out_specs=[...  143 us
    pallas_call x1, Pallas kernels, outputs(): pl.pallas_call(outputs_kernel, in_specs=[hbm, hbm, hbm, vmem], out_specs=...  5.2 us

profile of v2, /device:TPU:0, one launch (start us, length us, event | category | flops | bytes accessed | tf_op | source)
XLA Modules:
  0.0 148.9 jit_solution(823794773604898201)
XLA Ops:
  0.7 142.9 %whole_layer.1 = (bf16[1216,768]{1,0:T(8,128)(2,1)}, bf16[1216,768]{1,0:T(8,128)(2,1)}, f32[12,48,384]{2,1,0:T(8,128)}, f32[8,1536]{1,0:T(8,128)}, bf16[1216,153...) custom-call(bf16[1216,768]{1,0:T(8,128)(2,1)} %tok_h.1, bf16[1216,768]{1,0:T(8,128)(2,1)} %g_h.1, ...), custom_call_target="tpu_custom_call" | custom-call | flops 33999998976 | bytes 40000000 | tf_op jit(solution)/shard_map/whole_layer/pallas_call | solution.py:1057
  143.5 5.2 %outputs.1 = (bf16[1216,768]{1,0:T(8,128)(2,1)}, bf16[1216,768]{1,0:T(8,128)(2,1)}, f32[48]{0:T(128)}, f32[48]{0:T(128)}, f32[3,48,384]{2,1,0:T(8,128)}, /*index...) custom-call(bf16[1216,768]{1,0:T(8,128)(2,1)} %get-tuple-element.32., ...), custom_call_target="tpu_custom_call" | custom-call | tf_op jit(solution)/shard_map/outputs/pallas_call | solution.py:1163
